TPU v7x, 32 devices: a whole 2x2x4 slice. The times are simulated.
32 devices in a mesh: fsdp: 4 (over z), context: 2 (over y), tensor: 4 (over x, core).
Axes of the slice: x: 2, y: 2, z: 4, core: 2. Of those that a mesh axis runs over, the one named last changes fastest.
Arguments:
- tokens: bfloat16 [8, 4096, 768], P('fsdp', 'context'), may hold values from -6 to 6
- cotangent: bfloat16 [8, 4096, 768], P('fsdp', 'context'), may hold values from -6 to 6
- segments: int32 [8, 4096], P('fsdp'), may hold values from 0 to 4, as said below
- steps: int32 [8], P('fsdp'), may hold values from 0 to 255
- table: bfloat16 [256, 128], replicated, may hold values from -5 to 5
- ada_w: bfloat16 [128, 4608], replicated, may hold values from -0.5 to 0.5
- ada_b: bfloat16 [4608], replicated, may hold values from 0.099609375 to 1.8984375
- gain_one: bfloat16 [768], replicated, may hold values from 0.099609375 to 1.8984375
- w_qkv: bfloat16 [768, 2304], P('fsdp', 'tensor'), may hold values from -0.109375 to 0.109375
- w_out: bfloat16 [768, 768], P('tensor', 'fsdp'), may hold values from -3 to 3
- gain_two: bfloat16 [768], replicated, may hold values from 0.099609375 to 1.8984375
- w_up: bfloat16 [768, 3072], P('fsdp', 'tensor'), may hold values from -0.109375 to 0.109375
- b_up: bfloat16 [3072], replicated, may hold values from -3 to 3
- w_down: bfloat16 [3072, 768], P('tensor', 'fsdp'), may hold values from -0.15625 to 0.15625
- b_down: bfloat16 [768], replicated, may hold values from -3 to 3
Outputs:
- block_out: bfloat16 [8, 4096, 768], P('fsdp', 'context')
- grad_tokens: float32 [8, 4096, 768], P('fsdp', 'context', 'tensor')
- grad_table: float32 [256, 128], replicated
- grad_ada_w: float32 [128, 4608], replicated
- grad_ada_b: float32 [4608], replicated
- grad_gain_one: float32 [768], replicated
- grad_w_qkv: float32 [768, 2304], P('fsdp', 'tensor')
- grad_w_out: float32 [768, 768], P('tensor', 'fsdp')
- grad_gain_two: float32 [768], replicated
- grad_w_up: float32 [768, 3072], P('fsdp', 'tensor')
- grad_b_up: float32 [3072], replicated
- grad_w_down: float32 [3072, 768], P('tensor', 'fsdp')
- grad_b_down: float32 [768], replicated
Inputs may be any that keep to these rules, and one draw needn't show every extreme that they name: `segments`: along each sequence segment numbers never fall; 1 to 4 are its documents in order, each present, and 0 marks the padding at its end, present in every sequence. No document has more than 2048 tokens, and in every sequence one document has exactly 2048.
All inputs are finite; a program needn't handle non-finite values.
Results may differ from a plain program's by a relative error of at most 0.02.
Values may be sent and summed in bfloat16 or wider, within the bound.
A program may use at most 768 MiB of HBM per device.

v0:
```python
from functools import partial
import jax
import jax.numpy as jnp
from jax import lax
from jax.sharding import PartitionSpec as P

HDIM = 64
precise = lax.Precision.HIGHEST


def product(left_side, right_side):
    return jnp.dot(left_side, right_side, preferred_element_type=jnp.float32)


def transposed(left_side, right_side):
    return lax.dot_general(
        left_side, right_side, (((0,), (0,)), ((), ())), preferred_element_type=jnp.float32
    )


def against(left_side, right_side):
    return lax.dot_general(
        left_side, right_side, (((1,), (1,)), ((), ())), preferred_element_type=jnp.float32
    )


def exact_product(left_side, right_side):
    return jnp.dot(left_side, right_side, precision=precise, preferred_element_type=jnp.float32)


def exact_transposed(left_side, right_side):
    return lax.dot_general(
        left_side,
        right_side,
        (((0,), (0,)), ((), ())),
        precision=precise,
        preferred_element_type=jnp.float32,
    )


def exact_against(left_side, right_side):
    return lax.dot_general(
        left_side,
        right_side,
        (((1,), (1,)), ((), ())),
        precision=precise,
        preferred_element_type=jnp.float32,
    )


def normalize(operand):
    center = operand - jnp.mean(operand, axis=-1, keepdims=True)
    scaling = lax.rsqrt(jnp.mean(center * center, axis=-1, keepdims=True) + 1e-05)
    return (center * scaling, scaling)


def norm_back(grad_hat, hatted, scaling):
    return scaling * (
        grad_hat
        - jnp.mean(grad_hat, axis=-1, keepdims=True)
        - hatted * jnp.mean(grad_hat * hatted, axis=-1, keepdims=True)
    )


def positions(segment):
    indices = jnp.arange(segment.shape[0], dtype=jnp.int32)
    change = jnp.concatenate([jnp.ones((1,), jnp.bool_), segment[1:] != segment[:-1]])
    starts = lax.cummax(jnp.where(change, indices, 0), axis=0)
    return indices - starts


def angles_of(offsets, half_width):
    frequency = 10000.0 ** (-jnp.arange(half_width, dtype=jnp.float32) / half_width)
    angles = offsets.astype(jnp.float32)[:, None] * frequency[None, :]
    return (jnp.cos(angles)[:, None, :], jnp.sin(angles)[:, None, :])


def rotate(operand, cosine, sine_part, direction):
    half_width = operand.shape[-1] // 2
    front_half = operand[..., :half_width]
    second = operand[..., half_width:]
    return jnp.concatenate(
        [
            front_half * cosine - direction * second * sine_part,
            direction * front_half * sine_part + second * cosine,
        ],
        axis=-1,
    )


def scores_of(queries, key_rows, allowed):
    raw_scores = (
        jnp.einsum("qhd,khd->hqk", queries, key_rows, preferred_element_type=jnp.float32) * 0.125
    )
    return jnp.where(allowed[None], raw_scores, -1e30)


def attend(queries, key_rows, values, allowed):
    scores = scores_of(queries, key_rows, allowed)
    row_max = jnp.max(scores, axis=-1, keepdims=True)
    weights_raw = jnp.exp(scores - row_max)
    row_total = jnp.sum(weights_raw, axis=-1, keepdims=True)
    weights_low = (weights_raw / row_total).astype(jnp.bfloat16)
    mixture = jnp.einsum("hqk,khd->qhd", weights_low, values, preferred_element_type=jnp.float32)
    return (mixture, row_max + jnp.log(row_total))


def attend_back(queries, key_rows, values, grad_mixture, logsum, allowed, row_delta):
    scores = scores_of(queries, key_rows, allowed)
    chances = jnp.exp(scores - logsum)
    grad_chances = jnp.einsum(
        "qhd,khd->hqk", grad_mixture, values, preferred_element_type=jnp.float32
    )
    row_delta = jnp.sum(chances * grad_chances, axis=-1, keepdims=True)
    grad_scores = (chances * (grad_chances - row_delta)).astype(jnp.bfloat16)
    return (chances.astype(jnp.bfloat16), grad_scores, row_delta)


def local(
    tokens,
    cotangent,
    segments,
    steps,
    table,
    ada_w,
    ada_b,
    gain_one,
    w_qkv,
    w_out,
    gain_two,
    w_up,
    b_up,
    w_down,
    b_down,
):
    w_qkv, w_up, w_out, w_down = (
        lax.all_gather(w_qkv, "fsdp", axis=0, tiled=True),
        lax.all_gather(w_up, "fsdp", axis=0, tiled=True),
        lax.all_gather(w_out, "fsdp", axis=1, tiled=True),
        lax.all_gather(w_down, "fsdp", axis=1, tiled=True),
    )
    tensor_rank = lax.axis_index("tensor")
    context_rank = lax.axis_index("context")
    sequences, own_rows, model_width = tokens.shape
    length = segments.shape[1]
    local_heads = w_out.shape[0] // HDIM
    hidden_width = w_up.shape[1]
    up_bias = lax.dynamic_slice_in_dim(b_up, tensor_rank * hidden_width, hidden_width).astype(
        jnp.float32
    )
    down_bias = b_down.astype(jnp.float32)
    gain_first = gain_one.astype(jnp.float32)
    gain_second = gain_two.astype(jnp.float32)
    leader = (tensor_rank == 0).astype(jnp.float32)
    ada_full = ada_w.astype(jnp.float32)
    choose = (steps[:, None] == jnp.arange(table.shape[0], dtype=jnp.int32)[None, :]).astype(
        jnp.float32
    )
    before = exact_product(choose, table.astype(jnp.float32))
    embedding, silu_back = jax.vjp(jax.nn.silu, before)
    modulation = exact_product(embedding, ada_full) + ada_b.astype(jnp.float32)
    grad_qkv = jnp.zeros(w_qkv.shape, jnp.float32)
    grad_out_w = jnp.zeros(w_out.shape, jnp.float32)
    grad_up = jnp.zeros(w_up.shape, jnp.float32)
    grad_down = jnp.zeros(w_down.shape, jnp.float32)
    grad_bias_up = jnp.zeros((hidden_width,), jnp.float32)
    grad_bias_down = jnp.zeros((model_width,), jnp.float32)
    grad_gain_first = jnp.zeros((model_width,), jnp.float32)
    grad_gain_second = jnp.zeros((model_width,), jnp.float32)
    results = []
    partial_inputs = []
    carried = []
    grad_mods = []
    for number in range(sequences):
        shift_one, scale_one, gate_one, shift_two, scale_two, gate_two = jnp.split(
            modulation[number], 6
        )
        segment = segments[number]
        offsets = positions(segment)
        own_segment = lax.dynamic_slice_in_dim(segment, context_rank * own_rows, own_rows)
        own_offsets = lax.dynamic_slice_in_dim(offsets, context_rank * own_rows, own_rows)
        cosine, sine_part = angles_of(own_offsets, HDIM // 2)
        allowed = own_segment[:, None] == segment[None, :]
        inputs_row = tokens[number].astype(jnp.float32)
        hat_one, scaling_one = normalize(inputs_row)
        lifted_one = hat_one * gain_first
        entry_one = (lifted_one * (1.0 + scale_one) + shift_one).astype(jnp.bfloat16)
        projected = product(entry_one, w_qkv).reshape(own_rows, local_heads, 3, HDIM)
        queries = rotate(projected[:, :, 0], cosine, sine_part, 1.0).astype(jnp.bfloat16)
        key_rows = rotate(projected[:, :, 1], cosine, sine_part, 1.0).astype(jnp.bfloat16)
        values = projected[:, :, 2].astype(jnp.bfloat16)
        key_value = jnp.stack([key_rows, values], axis=1).reshape(own_rows, 2 * local_heads * HDIM)
        gathered = lax.all_gather(key_value, "context", axis=0, tiled=True).reshape(
            length, 2, local_heads, HDIM
        )
        all_keys = gathered[:, 0]
        all_values = gathered[:, 1]
        mixture, logsum = attend(queries, all_keys, all_values, allowed)
        mixture_low = mixture.reshape(own_rows, local_heads * HDIM).astype(jnp.bfloat16)
        attended = lax.psum(product(mixture_low, w_out).astype(jnp.bfloat16), "tensor").astype(
            jnp.float32
        )
        middle = inputs_row + gate_one * attended
        hat_two, scaling_two = normalize(middle)
        lifted_two = hat_two * gain_second
        entry_two = (lifted_two * (1.0 + scale_two) + shift_two).astype(jnp.bfloat16)
        hidden = product(entry_two, w_up) + up_bias
        activated, gelu_back = jax.vjp(partial(jax.nn.gelu, approximate=True), hidden)
        activated_low = activated.astype(jnp.bfloat16)
        output = (
            lax.psum(product(activated_low, w_down).astype(jnp.bfloat16), "tensor").astype(
                jnp.float32
            )
            + down_bias
        )
        results.append((middle + gate_two * output).astype(jnp.bfloat16))
        valid = (own_segment != 0).astype(jnp.float32)[:, None]
        grad_result = cotangent[number].astype(jnp.float32) * valid
        grad_output = (gate_two * grad_result).astype(jnp.bfloat16)
        grad_gate_two = jnp.sum(grad_result * output, axis=0)
        grad_bias_down = grad_bias_down + jnp.sum(grad_output.astype(jnp.float32), axis=0)
        grad_down = grad_down + transposed(activated_low, grad_output)
        grad_active = against(grad_output, w_down)
        grad_hidden = gelu_back(grad_active)[0].astype(jnp.bfloat16)
        grad_bias_up = grad_bias_up + jnp.sum(grad_hidden.astype(jnp.float32), axis=0)
        grad_up = grad_up + transposed(entry_two, grad_hidden)
        grad_entry_two = against(grad_hidden, w_up)
        grad_shift_two = jnp.sum(grad_entry_two, axis=0)
        grad_scale_two = jnp.sum(grad_entry_two * lifted_two, axis=0)
        grad_lifted_two = grad_entry_two * (1.0 + scale_two)
        grad_gain_second = grad_gain_second + jnp.sum(grad_lifted_two * hat_two, axis=0)
        part_two = norm_back(grad_lifted_two * gain_second, hat_two, scaling_two)
        grad_middle = grad_result + lax.psum(part_two.astype(jnp.bfloat16), "tensor").astype(
            jnp.float32
        )
        grad_attended = (gate_one * grad_middle).astype(jnp.bfloat16)
        grad_gate_one = jnp.sum(grad_middle * attended, axis=0)
        grad_out_w = grad_out_w + transposed(mixture_low, grad_attended)
        grad_mixture = (
            against(grad_attended, w_out).astype(jnp.bfloat16).reshape(own_rows, local_heads, HDIM)
        )
        chances_low, grad_scores, row_delta = attend_back(
            queries, all_keys, all_values, grad_mixture, logsum, allowed, None
        )
        grad_queries = (
            jnp.einsum("hqk,khd->qhd", grad_scores, all_keys, preferred_element_type=jnp.float32)
            * 0.125
        )
        grad_all_keys = (
            jnp.einsum("hqk,qhd->khd", grad_scores, queries, preferred_element_type=jnp.float32)
            * 0.125
        )
        grad_all_values = jnp.einsum(
            "hqk,qhd->khd", chances_low, grad_mixture, preferred_element_type=jnp.float32
        )
        both_grads = jnp.stack([grad_all_keys, grad_all_values], axis=1).reshape(
            length, 2 * local_heads * HDIM
        )
        own_grads = (
            lax.psum_scatter(
                both_grads.astype(jnp.bfloat16), "context", scatter_dimension=0, tiled=True
            )
            .astype(jnp.float32)
            .reshape(own_rows, 2, local_heads, HDIM)
        )
        grad_keys = own_grads[:, 0]
        grad_values = own_grads[:, 1]
        grad_queries = rotate(grad_queries, cosine, sine_part, -1.0)
        grad_keys = rotate(grad_keys, cosine, sine_part, -1.0)
        grad_projected = (
            jnp.stack([grad_queries, grad_keys, grad_values], axis=2)
            .reshape(own_rows, local_heads * 3 * HDIM)
            .astype(jnp.bfloat16)
        )
        grad_qkv = grad_qkv + transposed(entry_one, grad_projected)
        grad_entry_one = against(grad_projected, w_qkv)
        grad_shift_one = jnp.sum(grad_entry_one, axis=0)
        grad_scale_one = jnp.sum(grad_entry_one * lifted_one, axis=0)
        grad_lifted_one = grad_entry_one * (1.0 + scale_one)
        grad_gain_first = grad_gain_first + jnp.sum(grad_lifted_one * hat_one, axis=0)
        partial_inputs.append(norm_back(grad_lifted_one * gain_first, hat_one, scaling_one))
        carried.append(grad_middle)
        grad_mods.append(
            jnp.concatenate(
                [
                    grad_shift_one,
                    grad_scale_one,
                    grad_gate_one * leader,
                    grad_shift_two,
                    grad_scale_two,
                    grad_gate_two * leader,
                ]
            )
        )
    summed_inputs = lax.psum_scatter(
        jnp.stack(partial_inputs).astype(jnp.bfloat16), "tensor", scatter_dimension=2, tiled=True
    ).astype(jnp.float32)
    slice_width = model_width // lax.axis_size("tensor")
    own_middle = lax.dynamic_slice_in_dim(
        jnp.stack(carried), tensor_rank * slice_width, slice_width, axis=2
    )
    grad_tokens = summed_inputs + own_middle
    grad_mod = jnp.stack(grad_mods)
    bias_up_full = lax.dynamic_update_slice_in_dim(
        jnp.zeros((b_up.shape[0],), jnp.float32), grad_bias_up, tensor_rank * hidden_width, 0
    )
    grad_qkv, grad_up, grad_out_w, grad_down = (
        lax.psum_scatter(
            grad_qkv.astype(jnp.bfloat16), "fsdp", scatter_dimension=0, tiled=True
        ).astype(jnp.float32),
        lax.psum_scatter(
            grad_up.astype(jnp.bfloat16), "fsdp", scatter_dimension=0, tiled=True
        ).astype(jnp.float32),
        lax.psum_scatter(
            grad_out_w.astype(jnp.bfloat16), "fsdp", scatter_dimension=1, tiled=True
        ).astype(jnp.float32),
        lax.psum_scatter(
            grad_down.astype(jnp.bfloat16), "fsdp", scatter_dimension=1, tiled=True
        ).astype(jnp.float32),
    )
    grad_qkv, grad_up, grad_out_w, grad_down = (
        lax.psum(grad_qkv.astype(jnp.bfloat16), "context").astype(jnp.float32),
        lax.psum(grad_up.astype(jnp.bfloat16), "context").astype(jnp.float32),
        lax.psum(grad_out_w.astype(jnp.bfloat16), "context").astype(jnp.float32),
        lax.psum(grad_down.astype(jnp.bfloat16), "context").astype(jnp.float32),
    )
    grad_ada_b = jnp.sum(grad_mod, axis=0)
    grad_ada_w = exact_transposed(embedding, grad_mod)
    grad_embedding = exact_against(grad_mod, ada_full)
    grad_before = silu_back(grad_embedding)[0]
    grad_table = exact_transposed(choose, grad_before)
    (
        grad_table,
        grad_ada_w,
        grad_ada_b,
        grad_gain_first,
        grad_gain_second,
        bias_up_full,
        grad_bias_down,
    ) = lax.psum(
        (
            grad_table,
            grad_ada_w,
            grad_ada_b,
            grad_gain_first,
            grad_gain_second,
            bias_up_full,
            grad_bias_down * leader,
        ),
        ("fsdp", "context", "tensor"),
    )
    return (
        jnp.stack(results),
        grad_tokens,
        grad_table,
        grad_ada_w,
        grad_ada_b,
        grad_gain_first,
        grad_qkv,
        grad_out_w,
        grad_gain_second,
        grad_up,
        bias_up_full,
        grad_down,
        grad_bias_down,
    )


def solution(mesh):
    return jax.shard_map(
        local,
        mesh=mesh,
        in_specs=(
            P("fsdp", "context", None),
            P("fsdp", "context", None),
            P("fsdp", None),
            P("fsdp"),
            P(),
            P(),
            P(),
            P(),
            P("fsdp", "tensor"),
            P("tensor", "fsdp"),
            P(),
            P("fsdp", "tensor"),
            P(),
            P("tensor", "fsdp"),
            P(),
        ),
        out_specs=(
            P("fsdp", "context", None),
            P("fsdp", "context", "tensor"),
            P(),
            P(),
            P(),
            P(),
            P("fsdp", "tensor"),
            P("tensor", "fsdp"),
            P(),
            P("fsdp", "tensor"),
            P(),
            P("tensor", "fsdp"),
            P(),
        ),
        check_vma=False,
    )
```

profile of v0, /device:TPU:0, one launch (start us, length us, event | category | flops | bytes accessed | tf_op | source)
XLA Modules:
  0.0 1699.0 jit_solution(8537734256310967718)
XLA Ops:
  17.1 23.5 %all_gather.18 = bf16[768,576]{1,0:T(8,128)(2,1)S(1)} all-gather(bf16[192,576]{1,0:T(8,128)(2,1)S(1)} %copy-done.39), channel_id=1, replica_groups=mesh['fsdp'=4,'context'=2,'tensor'=4] {'fsdp'}, dimensions={0}, use_global_device_ids=true | all-gather | bytes 1105920 | tf_op jit(solution)/shard_map/all_gather | solution.py:137
  70.0 16.0 all_gather.20
  88.7 8.8 broadcast_compare_fusion.1
  97.5 16.4 all-gather.5.cloned.1.call-done
  113.9 37.9 %fusion.185 = (f32[3,2048]{1,0:T(4,128)S(1)}, f32[3,2048,4096]{2,1,0:T(8,128)}) fusion(bf16[4096,2,3,64]{0,3,2,1:T(8,128)(2,1)} %bitcast.367, bf16[2048,3,32]{0,2,1:T(8,128)(2,1)S(1)} %get-tuple-element.152, bf16[2048,3,32]{0,2,1:T(8,128)(2,1)S(1)} %get-tuple-element.151, pred[2048,4096]{1,0:T(8,128)(4,1)} %broadcast_compare_fusion.1), kind=kOutput, calls=%fused_computation.352 | convolution fusion | flops 3298289664 | bytes 111435776 | tf_op jit(solution)/shard_map/qhd,khd->hqk/dot_general | solution.py:93
  151.9 31.0 %fusion = f32[3,2048]{1,0:T(4,128)S(1)} fusion(f32[3,2048,4096]{2,1,0:T(8,128)} %get-tuple-element.175, f32[3,2048]{1,0:T(4,128)S(1)} %get-tuple-element.174), kind=kLoop, calls=%fused_computation.12 | loop fusion | flops 50325504 | bytes 100712448 | tf_op jit(solution)/shard_map/reduce_sum | solution.py:102
  182.9 33.9 %fusion.119 = bf16[3,64,2048]{2,1,0:T(8,128)(2,1)S(1)} fusion(f32[3,2048,4096]{2,1,0:T(8,128)} %get-tuple-element.175, f32[3,2048]{1,0:T(4,128)S(1)} %fusion, f32[3,2048]{1,0:T(4,128)S(1)} %get-tuple-element.174, bf16[4096,2,3,64]{0,3,2,1:T(8,128)(2,1)} %bitcast.368), kind=kOutput, calls=%fused_computation.184 | convolution fusion | flops 3297116160 | bytes 103071744 | tf_op jit(solution)/shard_map/hqk,khd->qhd/dot_general | solution.py:104
  219.7 68.5 %all-reduce.13.cloned.1.call-done = bf16[2048,768]{1,0:T(8,128)(2,1)} async-done(((bf16[2048,768]{1,0:T(8,128)(2,1)}), bf16[2048,768]{1,0:T(8,128)(2,1)}) %all-reduce.13.cloned.1.call-update) | async-done | bytes 3145744 | tf_op jit(solution)/shard_map/psum | solution.py:200
  288.3 5.6 fusion.105
  300.0 9.2 broadcast_compare_fusion
  309.3 35.7 %all-gather.11.cloned.1.call-done = bf16[4096,384]{0,1:T(8,128)(2,1)} async-done(((bf16[2048,384]{0,1:T(8,128)(2,1)}), bf16[4096,384]{0,1:T(8,128)(2,1)}) %all-gather.11.cloned.1.call-update) | async-done | bytes 3145744 | tf_op jit(solution)/shard_map/all_gather | solution.py:193
  345.0 37.4 %fusion.186 = (f32[3,2048]{1,0:T(4,128)S(1)}, f32[3,2048,4096]{2,1,0:T(8,128)}) fusion(bf16[4096,2,3,64]{0,3,2,1:T(8,128)(2,1)} %bitcast.371, bf16[2048,3,32]{0,2,1:T(8,128)(2,1)S(1)} %get-tuple-element.148, bf16[2048,3,32]{0,2,1:T(8,128)(2,1)S(1)} %get-tuple-element.147, pred[2048,4096]{1,0:T(8,128)(4,1)} %broadcast_compare_fusion), kind=kOutput, calls=%fused_computation.353 | convolution fusion | flops 3298289664 | bytes 111435776 | tf_op jit(solution)/shard_map/qhd,khd->hqk/dot_general | solution.py:93
  382.4 31.0 %fusion.1 = f32[3,2048]{1,0:T(4,128)S(1)} fusion(f32[3,2048,4096]{2,1,0:T(8,128)} %get-tuple-element.177, f32[3,2048]{1,0:T(4,128)S(1)} %get-tuple-element.176), kind=kLoop, calls=%fused_computation.13 | loop fusion | flops 50325504 | bytes 100712448 | tf_op jit(solution)/shard_map/reduce_sum | solution.py:102
  413.5 34.5 %fusion.118 = bf16[3,64,2048]{2,1,0:T(8,128)(2,1)} fusion(f32[3,2048,4096]{2,1,0:T(8,128)} %get-tuple-element.177, f32[3,2048]{1,0:T(4,128)S(1)} %fusion.1, f32[3,2048]{1,0:T(4,128)S(1)} %get-tuple-element.176, bf16[4096,2,3,64]{0,3,2,1:T(8,128)(2,1)} %bitcast.372), kind=kOutput, calls=%fused_computation.183 | convolution fusion | flops 3297116160 | bytes 103071744 | tf_op jit(solution)/shard_map/hqk,khd->qhd/dot_general | solution.py:104
  454.3 66.5 %all-reduce.15.cloned.1.call-done = bf16[2048,768]{1,0:T(8,128)(2,1)} async-done(((bf16[2048,768]{1,0:T(8,128)(2,1)}), bf16[2048,768]{1,0:T(8,128)(2,1)}) %all-reduce.15.cloned.1.call-update) | async-done | bytes 3145744 | tf_op jit(solution)/shard_map/psum | solution.py:200
  520.8 6.3 multiply_reduce_fusion.9
  529.5 9.8 multiply_convert_fusion.7
  539.3 10.3 convert_reduce_fusion.5
  556.7 8.3 convert_reduce_fusion.4
  565.1 12.1 multiply_reduce_fusion.2
  577.2 7.5 multiply_convert_fusion.3
  586.1 118.6 %all-reduce.21.cloned.1.call-done = (bf16[2048,768]{1,0:T(8,128)(2,1)}, bf16[2048,768]{1,0:T(8,128)(2,1)}) async-done(((bf16[2048,768]{1,0:T(8,128)(2,1)}, bf16[2048,768]{1,0:T(8,128)(2,1)}), (bf16[2048,768]{1,0:T(8,128)(2,1)}, bf16[2048,768]{1,0:T(8,128)(2,1)})) %all-reduce.21.cloned.1.call-update) | async-done | bytes 6291472 | tf_op jit(solution)/shard_map/psum | solution.py:233
  704.8 7.1 multiply_convert_fusion.4
  714.6 33.7 %fusion.86 = bf16[4096,1,3,64]{0,3,2,1:T(8,128)(2,1)} fusion(bf16[2048,3,64]{0,2,1:T(8,128)(2,1)S(1)} %bitcast.365, f32[3,2048,4096]{2,1,0:T(8,128)} %get-tuple-element.177, f32[3,2048]{1,0:T(4,128)S(1)} %log_add_fusion), kind=kOutput, calls=%fused_computation.145 | convolution fusion | flops 3272343552 | bytes 103047168 | tf_op jit(solution)/shard_map/hqk,qhd->khd/dot_general | solution.py:253
  748.4 65.7 %multiply_reduce_fusion = (f32[3,2048]{1,0:T(4,128)}, f32[3,2048,4096]{2,1,0:T(8,128)}) fusion(f32[3,2048,4096]{2,1,0:T(8,128)} %get-tuple-element.177, f32[3,2048]{1,0:T(4,128)} %copy-done.19, bf16[2048,3,64]{0,2,1:T(8,128)(2,1)S(1)} %bitcast.366, bf16[4096,2,3,64]{0,3,2,1:T(8,128)(2,1)} %bitcast.373), kind=kOutput, calls=%fused_computation.1 | convolution fusion | flops 3296716800 | bytes 203743232 | tf_op jit(solution)/shard_map/qhd,khd->hqk/dot_general | solution.py:111
  820.5 77.9 %multiply_convert_fusion = bf16[3,2048,4096]{2,1,0:T(8,128)(2,1)} fusion(f32[3,2048,4096]{2,1,0:T(8,128)} %get-tuple-element.184, f32[3,2048,4096]{2,1,0:T(8,128)} %get-tuple-element.177, f32[3,2048]{1,0:T(4,128)S(1)} %copy-done.45, f32[3,2048]{1,0:T(4,128)S(1)} %copy-done.20), kind=kLoop, calls=%fused_computation | loop fusion | flops 100663296 | bytes 251707392 | tf_op jit(solution)/shard_map/convert_element_type | solution.py:115
  898.3 21.3 %fusion.99 = bf16[4096,1,3,64]{0,3,2,1:T(8,128)(2,1)} fusion(bf16[3,2048,4096]{2,1,0:T(8,128)(2,1)} %multiply_convert_fusion, bf16[2048,3,32]{0,2,1:T(8,128)(2,1)S(1)} %copy-done.33, bf16[2048,3,32]{0,2,1:T(8,128)(2,1)S(1)} %copy-done.31), kind=kOutput, calls=%fused_computation.157 | convolution fusion | flops 3224371200 | bytes 52690944 | tf_op jit(solution)/shard_map/hqk,qhd->khd/dot_general | solution.py:250
  926.6 66.3 %multiply_reduce_fusion.1 = (f32[3,2048]{1,0:T(4,128)S(1)}, f32[3,2048,4096]{2,1,0:T(8,128)}) fusion(f32[3,2048,4096]{2,1,0:T(8,128)} %get-tuple-element.175, f32[3,2048]{1,0:T(4,128)S(1)} %copy-done.18, bf16[2048,3,64]{0,2,1:T(8,128)(2,1)S(1)} %bitcast.363, bf16[4096,2,3,64]{0,3,2,1:T(8,128)(2,1)} %bitcast.369), kind=kOutput, calls=%fused_computation.4 | convolution fusion | flops 3296716800 | bytes 203735040 | tf_op jit(solution)/shard_map/qhd,khd->hqk/dot_general | solution.py:111
  992.9 77.8 %multiply_convert_fusion.1 = bf16[3,2048,4096]{2,1,0:T(8,128)(2,1)} fusion(f32[3,2048,4096]{2,1,0:T(8,128)} %get-tuple-element.182, f32[3,2048,4096]{2,1,0:T(8,128)} %get-tuple-element.175, f32[3,2048]{1,0:T(4,128)S(1)} %get-tuple-element.181, f32[3,2048]{1,0:T(4,128)S(1)} %copy-done.18), kind=kLoop, calls=%fused_computation.3 | loop fusion | flops 100663296 | bytes 251707392 | tf_op jit(solution)/shard_map/convert_element_type | solution.py:115
  1070.7 21.2 %fusion.101 = bf16[4096,1,3,64]{0,3,2,1:T(8,128)(2,1)} fusion(bf16[3,2048,4096]{2,1,0:T(8,128)(2,1)} %multiply_convert_fusion.1, bf16[2048,3,32]{0,2,1:T(8,128)(2,1)S(1)} %copy-done.29, bf16[2048,3,32]{0,2,1:T(8,128)(2,1)S(1)} %copy-done.27), kind=kOutput, calls=%fused_computation.160 | convolution fusion | flops 3224371200 | bytes 52690944 | tf_op jit(solution)/shard_map/hqk,qhd->khd/dot_general | solution.py:250
  1091.9 32.6 %fusion.89 = bf16[4096,1,3,64]{0,3,2,1:T(8,128)(2,1)S(1)} fusion(bf16[2048,3,64]{0,2,1:T(8,128)(2,1)S(1)} %bitcast.364, f32[3,2048,4096]{2,1,0:T(8,128)} %get-tuple-element.175, f32[3,2048]{1,0:T(4,128)S(1)} %copy-done.18), kind=kOutput, calls=%fused_computation.146 | convolution fusion | flops 3272343552 | bytes 103047168 | tf_op jit(solution)/shard_map/hqk,qhd->khd/dot_general | solution.py:253
  1127.0 5.9 fusion.169
  1133.0 8.3 add_convert_fusion.4
  1141.7 7.4 fusion.130
  1149.2 6.7 add_convert_fusion.5
  1155.9 8.7 convolution_convert_fusion
  1168.8 22.7 %fusion.120 = f32[2048,3,64]{0,2,1:T(8,128)} fusion(bf16[3,2048,4096]{2,1,0:T(8,128)(2,1)} %multiply_convert_fusion, bf16[4096,2,3,64]{0,3,2,1:T(8,128)(2,1)} %bitcast.374), kind=kOutput, calls=%fused_computation.190 | convolution fusion | flops 3221618688 | bytes 53477376 | tf_op jit(solution)/shard_map/hqk,khd->qhd/dot_general | solution.py:246
  1191.6 22.0 %fusion.121 = f32[2048,3,64]{0,2,1:T(8,128)S(1)} fusion(bf16[3,2048,4096]{2,1,0:T(8,128)(2,1)} %multiply_convert_fusion.1, bf16[4096,2,3,64]{0,3,2,1:T(8,128)(2,1)} %bitcast.370), kind=kOutput, calls=%fused_computation.192 | convolution fusion | flops 3221618688 | bytes 53477376 | tf_op jit(solution)/shard_map/hqk,khd->qhd/dot_general | solution.py:246
  1237.5 12.7 fusion.42
  1250.3 14.0 reduce-scatter.13.cloned.1.call-done
  1264.4 9.6 fusion.109
  1277.2 16.5 copy.53
  1308.1 218.1 %all-reduce.19.cloned.1.call-done = (bf16[2048,768]{1,0:T(8,128)(2,1)}, bf16[2048,768]{1,0:T(8,128)(2,1)}, bf16[2,2048,768]{1,0,2:T(2,128)(2,1)}) async-done(((bf16[2048,768]{1,0:T(8,128)(2,1)}, bf16[2048,768]{1,0:T(8,128)(2,1)}, bf16[2,2048,768]{1,0,2:T(2,128)(2,1)}), (bf16[2048,768]{1,0:T(8,128)(2,1)}, bf16[2048,768]{1,0:T(8,128)(2,1)}, bf16[2,2048,768]{1,0,2:T(2,128)(2,1)})) %all-reduce.19.cloned.1.call-update) | async-done | bytes 12582928 | tf_op jit(solution)/shard_map/psum | solution.py:211
  1526.2 18.4 %convert_reduce_fusion.3 = (f32[768]{0:T(1024)S(1)}, f32[768]{0:T(1024)S(1)}, f32[768]{0:T(1024)S(1)}, f32[768]{0:T(1024)S(1)}, f32[768]{0:T(1024)S(1)}, /*index...) fusion(f32[2048]{0:T(1024)S(1)} %copy-done.53, ...), kind=kLoop, calls=%fused_computation.113 | loop fusion | flops 66055680 | bytes 50381824 | tf_op jit(solution)/shard_map/reduce_sum | solution.py:221
  1558.3 6.0 fusion.103
  1569.5 41.0 %all-reduce.1 = (f32[4608]{0:T(1024)}, f32[768]{0:T(1024)}, f32[768]{0:T(1024)}, f32[3072]{0:T(1024)}, f32[768]{0:T(1024)}) all-reduce(f32[4608]{0:T(1024)S(1)} %reduce_sum.399, f32[768]{0:T(1024)S(1)} %add.351, f32[768]{0:T(1024)S(1)} %add.354, ...), channel_id=1, replica_groups=mesh['fsdp'=4,'context'=2,'tensor'=4] {'fsdp','context','tensor'}, use_global_device_ids=true, to_apply=%region_49.50 | all-reduce | flops 9984 | bytes 79872 | tf_op jit(solution)/shard_map/psum | solution.py:340
  1610.6 6.1 pad_maximum_fusion
  1616.7 69.8 %all-reduce.17.cloned.1.call-done = (f32[256,128]{1,0:T(8,128)}, f32[128,4608]{1,0:T(8,128)}) async-done(((f32[256,128]{1,0:T(8,128)}, f32[128,4608]{1,0:T(8,128)}), (f32[256,128]{1,0:T(8,128)}, f32[128,4608]{1,0:T(8,128)})) %all-reduce.17.cloned.1.call-update) | async-done | bytes 2490384 | tf_op jit(solution)/shard_map/psum | solution.py:340
  (461 shorter events, 153.6 us)
Async XLA Ops:
  8.0 105.8 %all-gather.5.cloned.1.call-start = ((), (), s32[]{:S(2)}) async-start(), calls=%async_computation.6 | async-start | bytes 4718592 | tf_op jit(solution)/shard_map/all_gather | solution.py:193
  67.5 46.4 %copy-start.26 = (bf16[2048,3,32]{0,2,1:T(8,128)(2,1)}, bf16[2048,3,32]{0,2,1:T(8,128)(2,1)S(1)}, u32[]{:S(2)}) copy-start(bf16[2048,3,32]{0,2,1:T(8,128)(2,1)S(1)} %get-tuple-element.151) | copy-start | bytes 1179652
  67.5 46.4 %copy-start.28 = (bf16[2048,3,32]{0,2,1:T(8,128)(2,1)}, bf16[2048,3,32]{0,2,1:T(8,128)(2,1)S(1)}, u32[]{:S(2)}) copy-start(bf16[2048,3,32]{0,2,1:T(8,128)(2,1)S(1)} %get-tuple-element.152) | copy-start | bytes 1179652
  68.9 219.3 %all-reduce.13.cloned.1.call-start = ((), (), s32[]{:S(2)}) async-start(), calls=%async_computation.7 | async-start | bytes 6291456 | tf_op jit(solution)/shard_map/psum | solution.py:200
  182.9 34.0 %copy-start.8 = (bf16[192,768]{0,1:T(8,128)(2,1)S(1)}, bf16[192,768]{0,1:T(8,128)(2,1)}, u32[]{:S(2)}) copy-start(bf16[192,768]{0,1:T(8,128)(2,1)} %all_gather.20) | copy-start | bytes 884740
  216.9 71.4 %copy-start.40 = (f32[768]{0:T(1024)S(1)}, f32[768]{0:T(1024)}, u32[]{:S(2)}) copy-start(f32[768]{0:T(1024)} %get-tuple-element.104) | copy-start | bytes 9220
  216.9 71.4 %copy-start.57 = (f32[2048]{0:T(1024)S(1)}, f32[2048]{0:T(1024)}, u32[]{:S(2)}) copy-start(f32[2048]{0:T(1024)} %get-tuple-element.190) | copy-start | bytes 24580
  219.6 74.8 %slice-start = ((s8[6291456]{0:T(1024)(128)(4,1)}), s8[2097152]{0:T(1024)(128)(4,1)S(1)}, s32[]{:S(2)}) async-start(s8[6291456]{0:T(1024)(128)(4,1)} %bitcast.351), calls=%async_computation.22 | async-start | bytes 4194304
  219.6 74.8 %copy-start.79 = (f32[768]{0:T(1024)S(1)}, f32[768]{0:T(1024)}, u32[]{:S(2)}) copy-start(f32[768]{0:T(1024)} %copy-done.78) | copy-start | bytes 9220
  219.6 74.8 %copy-start.87 = (f32[768]{0:T(1024)S(1)}, f32[768]{0:T(1024)}, u32[]{:S(2)}) copy-start(f32[768]{0:T(1024)} %get-tuple-element.98) | copy-start | bytes 9220
  219.6 74.8 %copy-start.112 = (f32[768]{0:T(1024)S(1)}, f32[768]{0:T(1024)}, u32[]{:S(2)}) copy-start(f32[768]{0:T(1024)} %get-tuple-element.97) | copy-start | bytes 9220
  219.7 125.3 %all-gather.11.cloned.1.call-start = ((), (), s32[]{:S(2)}) async-start(), calls=%async_computation.10 | async-start | bytes 4718592 | tf_op jit(solution)/shard_map/all_gather | solution.py:193
  298.4 46.6 %copy-start.30 = (bf16[2048,3,32]{0,2,1:T(8,128)(2,1)}, bf16[2048,3,32]{0,2,1:T(8,128)(2,1)S(1)}, u32[]{:S(2)}) copy-start(bf16[2048,3,32]{0,2,1:T(8,128)(2,1)S(1)} %get-tuple-element.147) | copy-start | bytes 1179652
  298.4 46.6 %copy-start.32 = (bf16[2048,3,32]{0,2,1:T(8,128)(2,1)}, bf16[2048,3,32]{0,2,1:T(8,128)(2,1)S(1)}, u32[]{:S(2)}) copy-start(bf16[2048,3,32]{0,2,1:T(8,128)(2,1)S(1)} %get-tuple-element.148) | copy-start | bytes 1179652
  299.8 221.0 %all-reduce.15.cloned.1.call-start = ((), (), s32[]{:S(2)}) async-start(), calls=%async_computation.11 | async-start | bytes 6291456 | tf_op jit(solution)/shard_map/psum | solution.py:200
  448.0 72.8 %copy-start.41 = (f32[768]{0:T(1024)S(1)}, f32[768]{0:T(1024)}, u32[]{:S(2)}) copy-start(f32[768]{0:T(1024)} %get-tuple-element.104) | copy-start | bytes 9220
  448.0 72.8 %copy-start.43 = (f32[768]{0:T(1024)S(1)}, f32[768]{0:T(1024)}, u32[]{:S(2)}) copy-start(f32[768]{0:T(1024)} %get-tuple-element.99) | copy-start | bytes 9220
  448.1 79.2 %slice-start.2 = ((s8[6291456]{0:T(1024)(128)(4,1)}), s8[2097152]{0:T(1024)(128)(4,1)S(1)}, s32[]{:S(2)}) async-start(s8[6291456]{0:T(1024)(128)(4,1)} %bitcast.353), calls=%async_computation.24 | async-start | bytes 4194304
  452.2 77.2 %all-gather.7.cloned.1.call-start = ((), (), s32[]{:S(2)}) async-start(), calls=%async_computation.8 | async-start | bytes 1474560 | tf_op jit(solution)/shard_map/all_gather | solution.py:138
  452.8 86.5 %all-gather.9.cloned.1.call-start = ((), (), s32[]{:S(2)}) async-start(), calls=%async_computation.9 | async-start | bytes 1474560 | tf_op jit(solution)/shard_map/all_gather | solution.py:140
  453.4 251.4 %all-reduce.21.cloned.1.call-start = ((), (), s32[]{:S(2)}) async-start(), calls=%async_computation.20 | async-start | bytes 12582912 | tf_op jit(solution)/shard_map/psum | solution.py:233
  453.4 251.3 %copy-start.52 = (f32[2048]{0:T(1024)}, f32[2048]{0:T(1024)S(1)}, u32[]{:S(2)}) copy-start(f32[2048]{0:T(1024)S(1)} %compare_convert_fusion.1) | copy-start | bytes 24580
  453.5 251.3 %copy-start.54 = (f32[2048]{0:T(1024)}, f32[2048]{0:T(1024)S(1)}, u32[]{:S(2)}) copy-start(f32[2048]{0:T(1024)S(1)} %compare_convert_fusion) | copy-start | bytes 24580
  453.5 123.6 %copy-start.91 = (f32[768]{0:T(1024)}, f32[768]{0:T(1024)S(1)}, u32[]{:S(2)}) copy-start(f32[768]{0:T(1024)S(1)} %convert_element_type.335) | copy-start | bytes 9220
  454.3 102.4 %copy-start.108 = (f32[768]{0:T(1024)}, f32[768]{0:T(1024)S(1)}, u32[]{:S(2)}) copy-start(f32[768]{0:T(1024)S(1)} %dynamic-slice_convert_fusion) | copy-start | bytes 9220
  454.3 122.8 %copy-start.65 = (f32[2048]{0:T(1024)}, f32[2048]{0:T(1024)S(1)}, u32[]{:S(2)}) copy-start(f32[2048]{0:T(1024)S(1)} %broadcast_multiply_fusion.12) | copy-start | bytes 24580
  527.7 49.5 %copy-start.67 = (f32[2048]{0:T(1024)}, f32[2048]{0:T(1024)S(1)}, u32[]{:S(2)}) copy-start(f32[2048]{0:T(1024)S(1)} %broadcast_multiply_fusion.10) | copy-start | bytes 24580
  529.4 47.8 %copy-start.76 = (f32[2048]{0:T(1024)}, f32[2048]{0:T(1024)S(1)}, u32[]{:S(2)}) copy-start(f32[2048]{0:T(1024)S(1)} %add_rsqrt_fusion.2) | copy-start | bytes 24580
  529.4 47.8 %copy-start.74 = (f32[2048]{0:T(1024)}, f32[2048]{0:T(1024)S(1)}, u32[]{:S(2)}) copy-start(f32[2048]{0:T(1024)S(1)} %add_rsqrt_fusion) | copy-start | bytes 24580
  584.7 628.9 %reduce-scatter.19.cloned.1.call-start = ((), (), s32[]{:S(2)}) async-start(), calls=%async_computation.17 | async-start | bytes 491520
  586.1 128.5 %copy-start.19 = (f32[3,2048]{1,0:T(4,128)}, f32[3,2048]{1,0:T(4,128)S(1)}, u32[]{:S(2)}) copy-start(f32[3,2048]{1,0:T(4,128)S(1)} %log_add_fusion) | copy-start | bytes 73732
  748.4 65.7 %copy-start.17 = (bf16[3,64,2048]{2,1,0:T(8,128)(2,1)S(1)}, bf16[3,64,2048]{2,1,0:T(8,128)(2,1)}, u32[]{:S(2)}) copy-start(bf16[3,64,2048]{2,1,0:T(8,128)(2,1)} %copy-done.16) | copy-start | bytes 2359300
  748.4 68.4 %copy-start.15 = (bf16[3,64,2048]{2,1,0:T(8,128)(2,1)S(1)}, bf16[3,64,2048]{2,1,0:T(8,128)(2,1)}, u32[]{:S(2)}) copy-start(bf16[3,64,2048]{2,1,0:T(8,128)(2,1)} %fusion.118) | copy-start | bytes 2359300
  820.4 394.9 %reduce-scatter.11.cloned.1.call-start = ((), (), s32[]{:S(2)}) async-start(), calls=%async_computation.13 | async-start | bytes 4718592 | tf_op jit(solution)/shard_map/reduce_scatter | solution.py:260
  820.4 77.9 %copy-start.31 = (bf16[2048,3,32]{0,2,1:T(8,128)(2,1)S(1)}, bf16[2048,3,32]{0,2,1:T(8,128)(2,1)}, u32[]{:S(2)}) copy-start(bf16[2048,3,32]{0,2,1:T(8,128)(2,1)} %copy-done.30) | copy-start | bytes 1179652
  820.5 77.9 %copy-start.33 = (bf16[2048,3,32]{0,2,1:T(8,128)(2,1)S(1)}, bf16[2048,3,32]{0,2,1:T(8,128)(2,1)}, u32[]{:S(2)}) copy-start(bf16[2048,3,32]{0,2,1:T(8,128)(2,1)} %copy-done.32) | copy-start | bytes 1179652
  926.5 291.9 %reduce-scatter.9.cloned.1.call-start = ((), (), s32[]{:S(2)}) async-start(), calls=%async_computation.12 | async-start | bytes 4718592 | tf_op jit(solution)/shard_map/reduce_scatter | solution.py:260
  992.9 77.8 %copy-start.27 = (bf16[2048,3,32]{0,2,1:T(8,128)(2,1)S(1)}, bf16[2048,3,32]{0,2,1:T(8,128)(2,1)}, u32[]{:S(2)}) copy-start(bf16[2048,3,32]{0,2,1:T(8,128)(2,1)} %copy-done.26) | copy-start | bytes 1179652
  992.9 77.8 %copy-start.29 = (bf16[2048,3,32]{0,2,1:T(8,128)(2,1)S(1)}, bf16[2048,3,32]{0,2,1:T(8,128)(2,1)}, u32[]{:S(2)}) copy-start(bf16[2048,3,32]{0,2,1:T(8,128)(2,1)} %copy-done.28) | copy-start | bytes 1179652
  1126.5 123.8 %reduce-scatter.17.cloned.1.call-start = ((), (), s32[]{:S(2)}) async-start(), calls=%async_computation.16 | async-start | bytes 1474560 | tf_op jit(solution)/shard_map/reduce_scatter | solution.py:317
  1141.4 108.9 %reduce-scatter.15.cloned.1.call-start = ((), (), s32[]{:S(2)}) async-start(), calls=%async_computation.15 | async-start | bytes 1474560 | tf_op jit(solution)/shard_map/reduce_scatter | solution.py:311
  1155.9 108.4 %reduce-scatter.13.cloned.1.call-start = ((), (), s32[]{:S(2)}) async-start(), calls=%async_computation.14 | async-start | bytes 1228800 | tf_op jit(solution)/shard_map/reduce_scatter | solution.py:308
  1237.4 63.7 %all-reduce.23.cloned.1.call-start = ((), (), s32[]{:S(2)}) async-start(), calls=%async_computation.21 | async-start | bytes 1867776 | tf_op jit(solution)/shard_map/psum | solution.py:322
  1264.3 261.9 %all-reduce.19.cloned.1.call-start = ((), (), s32[]{:S(2)}) async-start(), calls=%async_computation.19 | async-start | bytes 25165824 | tf_op jit(solution)/shard_map/psum | solution.py:211
  1293.7 232.4 %copy-start.56 = (f32[2048]{0:T(1024)S(1)}, f32[2048]{0:T(1024)}, u32[]{:S(2)}) copy-start(f32[2048]{0:T(1024)} %copy-done.54) | copy-start | bytes 24580
  1293.8 232.4 %copy-start.83 = (f32[768]{0:T(1024)S(1)}, f32[768]{0:T(1024)}, u32[]{:S(2)}) copy-start(f32[768]{0:T(1024)} %get-tuple-element.93) | copy-start | bytes 9220
  1293.8 232.4 %copy-start.86 = (f32[768]{0:T(1024)S(1)}, f32[768]{0:T(1024)}, u32[]{:S(2)}) copy-start(f32[768]{0:T(1024)} %get-tuple-element.96) | copy-start | bytes 9220
  1293.8 392.7 %all-reduce.17.cloned.1.call-start = ((), (), s32[]{:S(2)}) async-start(), calls=%async_computation.18 | async-start | bytes 4980736 | tf_op jit(solution)/shard_map/psum | solution.py:340
  (111 other events, 886.9 us)
Sparse Core Ops, SparseCore 0:
  69.1 44.7 all-gather.4
  219.8 68.4 all-reduce.12
  299.9 45.0 all-gather.10
  452.3 68.4 all-reduce.14
  584.8 119.8 all-reduce.20
  1264.4 36.6 all-reduce.22
  1304.7 221.4 all-reduce.18
  1550.6 135.9 all-reduce.16
Sparse Core Ops, SparseCore 1:
  454.2 30.2 all-gather.6
  485.9 29.4 all-gather.8
  820.5 20.8 reduce-scatter.18
  926.6 43.5 reduce-scatter.10
  1126.6 43.4 reduce-scatter.8
  1172.5 29.2 reduce-scatter.16
  1204.0 27.8 reduce-scatter.14
  1237.5 26.7 reduce-scatter.12
where the time goes:
time: 1710 us; the launch traced here: 1700 us
  waiting for transfers between devices  614 us (36%)
  matrix products  573 us (34%)
  other arithmetic  354 us (21%)
  blocking collectives  80.5 us (5%)
  local copies, waits for them, and re-layouts  56.9 us (3%)
  between operations  18.7 us (1%)
    psum x1, waiting for transfers between devices, local(): lax.psum(product(activated_low, w_down).astype(jnp.bfloat16), 'tensor')  218 us
    convert_element_type x2, other arithmetic, attend_back(): grad_scores = (chances * (grad_chances - row_delta)).astype(jnp.bfloat16)  156 us
    psum x2, waiting for transfers between devices, local(): lax.psum(product(mixture_low, w_out).astype(jnp.bfloat16), 'tensor')  135 us
    dot_general x2, matrix products, attend_back(): jnp.einsum('qhd,khd->hqk', grad_mixture, values, preferred_element_type=j...  132 us
    psum x1, waiting for transfers between devices, local(): lax.psum(part_two.astype(jnp.bfloat16), 'tensor').astype(jnp.float32)  119 us
    dot_general x2, matrix products, scores_of(): jnp.einsum('qhd,khd->hqk', queries, key_rows, preferred_element_type=jnp....  75.4 us
    psum x1, waiting for transfers between devices, local(): lax.psum((grad_table, grad_ada_w, grad_ada_b, grad_gain_first, grad_gain_...  69.8 us
    dot_general x2, matrix products, attend(): jnp.einsum('hqk,khd->qhd', weights_low, values, preferred_element_type=jn...  68.5 us
  transfers between devices with their start and end apart: 16, of which 9 were waited for; matrix products, arithmetic and copies ran while one was open for 31% of the time, Pallas kernels for 0%

commit v1 on v0

--- a/solution.py
+++ b/solution.py
@@ -338,16 +338,19 @@
         bias_up_full,
         grad_bias_down,
     ) = lax.psum(
-        (
-            grad_table,
-            grad_ada_w,
-            grad_ada_b,
-            grad_gain_first,
-            grad_gain_second,
-            bias_up_full,
-            grad_bias_down * leader,
+        lax.psum(
+            (
+                grad_table,
+                grad_ada_w,
+                grad_ada_b,
+                grad_gain_first,
+                grad_gain_second,
+                bias_up_full,
+                grad_bias_down * leader,
+            ),
+            ("context", "tensor"),
         ),
-        ("fsdp", "context", "tensor"),
+        "fsdp",
     )
     return (
         jnp.stack(results),

time: 1710 us -> 1680 us (0.982)
  waiting for transfers between devices: 614 us -> 591 us
    psum x1, waiting for transfers between devices: 218 us -> 173 us  [local(): lax.psum(product(activated_low, w_down).astype(jnp.bfloat16), 'tensor')]
    psum x1, waiting for transfers between devices: 5.22 us -> 38.9 us  [local(): lax.psum(grad_qkv.astype(jnp.bfloat16), 'context').astype(jnp.float32)]
    psum x0 -> x1, waiting for transfers between devices: none -> 25.4 us  [local(): lax.psum(lax.psum((grad_table, grad_ada_w, grad_ada_b, grad_gain_first, g...]
    psum x0 -> x1, blocking collectives: none -> 20.7 us  [local(): lax.psum(lax.psum((grad_table, grad_ada_w, grad_ada_b, grad_gain_first, g...]
  transfers between devices with their start and end apart: 16 -> 17, of which waited for: 9 -> 9; matrix products, arithmetic and copies ran while one was open for 31% -> 24% of each run, Pallas kernels for 0% -> 0%
where the time goes in v1:
time: 1680 us
  waiting for transfers between devices  591 us (35%)
  matrix products  572 us (34%)
  other arithmetic  350 us (21%)
  blocking collectives  84.8 us (5%)
  local copies, waits for them, and re-layouts  56.8 us (3%)
  between operations  19 us (1%)
    psum x1, waiting for transfers between devices, local(): lax.psum(product(activated_low, w_down).astype(jnp.bfloat16), 'tensor')  173 us
    convert_element_type x2, other arithmetic, attend_back(): grad_scores = (chances * (grad_chances - row_delta)).astype(jnp.bfloat16)  155 us
    psum x2, waiting for transfers between devices, local(): lax.psum(product(mixture_low, w_out).astype(jnp.bfloat16), 'tensor')  135 us
    dot_general x2, matrix products, attend_back(): jnp.einsum('qhd,khd->hqk', grad_mixture, values, preferred_element_type=j...  132 us
    psum x1, waiting for transfers between devices, local(): lax.psum(part_two.astype(jnp.bfloat16), 'tensor').astype(jnp.float32)  103 us
    dot_general x2, matrix products, scores_of(): jnp.einsum('qhd,khd->hqk', queries, key_rows, preferred_element_type=jnp....  75 us
    dot_general x2, matrix products, attend(): jnp.einsum('hqk,khd->qhd', weights_low, values, preferred_element_type=jn...  68.4 us
    dot_general x2, matrix products, local(): jnp.einsum('hqk,qhd->khd', chances_low, grad_mixture, preferred_element_t...  66.3 us
  transfers between devices with their start and end apart: 17, of which 9 were waited for; matrix products, arithmetic and copies ran while one was open for 24% of the time, Pallas kernels for 0%

profile of v1, /device:TPU:0, one launch (start us, length us, event | category | flops | bytes accessed | tf_op | source)
XLA Modules:
  0.0 1675.6 jit_solution(6222309052467722727)
XLA Ops:
  17.1 23.5 %all_gather.18 = bf16[768,576]{1,0:T(8,128)(2,1)S(1)} all-gather(bf16[192,576]{1,0:T(8,128)(2,1)S(1)} %copy-done.37), channel_id=1, replica_groups=mesh['fsdp'=4,'context'=2,'tensor'=4] {'fsdp'}, dimensions={0}, use_global_device_ids=true | all-gather | bytes 1105920 | tf_op jit(solution)/shard_map/all_gather | solution.py:137
  70.0 16.3 all_gather.20
  88.9 8.8 broadcast_compare_fusion.1
  97.8 16.1 all-gather.5.cloned.1.call-done
  113.9 37.6 %fusion.185 = (f32[3,2048]{1,0:T(4,128)S(1)}, f32[3,2048,4096]{2,1,0:T(8,128)}) fusion(bf16[4096,2,3,64]{0,3,2,1:T(8,128)(2,1)} %bitcast.365, bf16[2048,3,32]{0,2,1:T(8,128)(2,1)S(1)} %get-tuple-element.159, bf16[2048,3,32]{0,2,1:T(8,128)(2,1)S(1)} %get-tuple-element.158, pred[2048,4096]{1,0:T(8,128)(4,1)} %broadcast_compare_fusion.1), kind=kOutput, calls=%fused_computation.352 | convolution fusion | flops 3298289664 | bytes 111435776 | tf_op jit(solution)/shard_map/qhd,khd->hqk/dot_general | solution.py:93
  151.5 31.0 %fusion = f32[3,2048]{1,0:T(4,128)S(1)} fusion(f32[3,2048,4096]{2,1,0:T(8,128)} %get-tuple-element.182, f32[3,2048]{1,0:T(4,128)S(1)} %get-tuple-element.181), kind=kLoop, calls=%fused_computation.12 | loop fusion | flops 50325504 | bytes 100712448 | tf_op jit(solution)/shard_map/reduce_sum | solution.py:102
  182.5 33.8 %fusion.119 = bf16[3,64,2048]{2,1,0:T(8,128)(2,1)S(1)} fusion(f32[3,2048,4096]{2,1,0:T(8,128)} %get-tuple-element.182, f32[3,2048]{1,0:T(4,128)S(1)} %fusion, f32[3,2048]{1,0:T(4,128)S(1)} %get-tuple-element.181, bf16[4096,2,3,64]{0,3,2,1:T(8,128)(2,1)} %bitcast.366), kind=kOutput, calls=%fused_computation.184 | convolution fusion | flops 3297116160 | bytes 103071744 | tf_op jit(solution)/shard_map/hqk,khd->qhd/dot_general | solution.py:104
  219.2 68.5 %all-reduce.16.cloned.1.call-done = bf16[2048,768]{1,0:T(8,128)(2,1)} async-done(((bf16[2048,768]{1,0:T(8,128)(2,1)}), bf16[2048,768]{1,0:T(8,128)(2,1)}) %all-reduce.16.cloned.1.call-update) | async-done | bytes 3145744 | tf_op jit(solution)/shard_map/psum | solution.py:200
  299.5 9.2 broadcast_compare_fusion
  308.8 35.7 %all-gather.11.cloned.1.call-done = bf16[4096,384]{0,1:T(8,128)(2,1)} async-done(((bf16[2048,384]{0,1:T(8,128)(2,1)}), bf16[4096,384]{0,1:T(8,128)(2,1)}) %all-gather.11.cloned.1.call-update) | async-done | bytes 3145744 | tf_op jit(solution)/shard_map/all_gather | solution.py:193
  344.4 37.4 %fusion.186 = (f32[3,2048]{1,0:T(4,128)S(1)}, f32[3,2048,4096]{2,1,0:T(8,128)}) fusion(bf16[4096,2,3,64]{0,3,2,1:T(8,128)(2,1)} %bitcast.369, bf16[2048,3,32]{0,2,1:T(8,128)(2,1)S(1)} %get-tuple-element.155, bf16[2048,3,32]{0,2,1:T(8,128)(2,1)S(1)} %get-tuple-element.154, pred[2048,4096]{1,0:T(8,128)(4,1)} %broadcast_compare_fusion), kind=kOutput, calls=%fused_computation.353 | convolution fusion | flops 3298289664 | bytes 111435776 | tf_op jit(solution)/shard_map/qhd,khd->hqk/dot_general | solution.py:93
  381.9 31.0 %fusion.1 = f32[3,2048]{1,0:T(4,128)S(1)} fusion(f32[3,2048,4096]{2,1,0:T(8,128)} %get-tuple-element.184, f32[3,2048]{1,0:T(4,128)S(1)} %get-tuple-element.183), kind=kLoop, calls=%fused_computation.13 | loop fusion | flops 50325504 | bytes 100712448 | tf_op jit(solution)/shard_map/reduce_sum | solution.py:102
  412.9 34.6 %fusion.118 = bf16[3,64,2048]{2,1,0:T(8,128)(2,1)} fusion(f32[3,2048,4096]{2,1,0:T(8,128)} %get-tuple-element.184, f32[3,2048]{1,0:T(4,128)S(1)} %fusion.1, f32[3,2048]{1,0:T(4,128)S(1)} %get-tuple-element.183, bf16[4096,2,3,64]{0,3,2,1:T(8,128)(2,1)} %bitcast.370), kind=kOutput, calls=%fused_computation.183 | convolution fusion | flops 3297116160 | bytes 103071744 | tf_op jit(solution)/shard_map/hqk,khd->qhd/dot_general | solution.py:104
  453.8 66.5 %all-reduce.18.cloned.1.call-done = bf16[2048,768]{1,0:T(8,128)(2,1)} async-done(((bf16[2048,768]{1,0:T(8,128)(2,1)}), bf16[2048,768]{1,0:T(8,128)(2,1)}) %all-reduce.18.cloned.1.call-update) | async-done | bytes 3145744 | tf_op jit(solution)/shard_map/psum | solution.py:200
  520.3 6.6 multiply_reduce_fusion.9
  529.0 9.8 multiply_convert_fusion.7
  538.8 10.1 convert_reduce_fusion.5
  556.0 8.3 convert_reduce_fusion.4
  564.3 12.1 multiply_reduce_fusion.2
  576.4 7.5 multiply_convert_fusion.3
  585.3 6.7 convolution_convert_fusion.1
  592.0 8.5 convolution_convert_fusion
  600.6 103.4 %all-reduce.26.cloned.1.call-done = (bf16[2048,768]{1,0:T(8,128)(2,1)}, bf16[2048,768]{1,0:T(8,128)(2,1)}) async-done(((bf16[2048,768]{1,0:T(8,128)(2,1)}, bf16[2048,768]{1,0:T(8,128)(2,1)}), (bf16[2048,768]{1,0:T(8,128)(2,1)}, bf16[2048,768]{1,0:T(8,128)(2,1)})) %all-reduce.26.cloned.1.call-update) | async-done | bytes 6291472 | tf_op jit(solution)/shard_map/psum | solution.py:233
  704.0 7.0 multiply_convert_fusion.4
  713.8 33.7 %fusion.86 = bf16[4096,1,3,64]{0,3,2,1:T(8,128)(2,1)} fusion(bf16[2048,3,64]{0,2,1:T(8,128)(2,1)S(1)} %bitcast.363, f32[3,2048,4096]{2,1,0:T(8,128)} %get-tuple-element.184, f32[3,2048]{1,0:T(4,128)S(1)} %log_add_fusion), kind=kOutput, calls=%fused_computation.145 | convolution fusion | flops 3272343552 | bytes 103047168 | tf_op jit(solution)/shard_map/hqk,qhd->khd/dot_general | solution.py:253
  747.5 64.7 %multiply_reduce_fusion = (f32[3,2048]{1,0:T(4,128)S(1)}, f32[3,2048,4096]{2,1,0:T(8,128)}) fusion(f32[3,2048,4096]{2,1,0:T(8,128)} %get-tuple-element.184, f32[3,2048]{1,0:T(4,128)S(1)} %log_add_fusion, bf16[2048,3,64]{0,2,1:T(8,128)(2,1)S(1)} %bitcast.364, bf16[4096,2,3,64]{0,3,2,1:T(8,128)(2,1)} %bitcast.371), kind=kOutput, calls=%fused_computation.1 | convolution fusion | flops 3296716800 | bytes 203735040 | tf_op jit(solution)/shard_map/qhd,khd->hqk/dot_general | solution.py:111
  815.3 77.7 %multiply_convert_fusion = bf16[3,2048,4096]{2,1,0:T(8,128)(2,1)} fusion(f32[3,2048,4096]{2,1,0:T(8,128)} %get-tuple-element.191, f32[3,2048,4096]{2,1,0:T(8,128)} %get-tuple-element.184, f32[3,2048]{1,0:T(4,128)S(1)} %get-tuple-element.190, f32[3,2048]{1,0:T(4,128)S(1)} %log_add_fusion), kind=kLoop, calls=%fused_computation | loop fusion | flops 100663296 | bytes 251707392 | tf_op jit(solution)/shard_map/convert_element_type | solution.py:115
  893.0 21.5 %fusion.99 = bf16[4096,1,3,64]{0,3,2,1:T(8,128)(2,1)} fusion(bf16[3,2048,4096]{2,1,0:T(8,128)(2,1)} %multiply_convert_fusion, bf16[2048,3,32]{0,2,1:T(8,128)(2,1)} %copy-done.31, bf16[2048,3,32]{0,2,1:T(8,128)(2,1)} %copy-done.30), kind=kOutput, calls=%fused_computation.157 | convolution fusion | flops 3224371200 | bytes 52690944 | tf_op jit(solution)/shard_map/hqk,qhd->khd/dot_general | solution.py:250
  917.9 67.6 %multiply_reduce_fusion.1 = (f32[3,2048]{1,0:T(4,128)S(1)}, f32[3,2048,4096]{2,1,0:T(8,128)}) fusion(f32[3,2048,4096]{2,1,0:T(8,128)} %get-tuple-element.182, f32[3,2048]{1,0:T(4,128)} %log_add_fusion.1, bf16[2048,3,64]{0,2,1:T(8,128)(2,1)S(1)} %bitcast.361, bf16[4096,2,3,64]{0,3,2,1:T(8,128)(2,1)} %bitcast.367), kind=kOutput, calls=%fused_computation.4 | convolution fusion | flops 3296716800 | bytes 203743232 | tf_op jit(solution)/shard_map/qhd,khd->hqk/dot_general | solution.py:111
  985.5 77.7 %multiply_convert_fusion.1 = bf16[3,2048,4096]{2,1,0:T(8,128)(2,1)} fusion(f32[3,2048,4096]{2,1,0:T(8,128)} %get-tuple-element.189, f32[3,2048,4096]{2,1,0:T(8,128)} %get-tuple-element.182, f32[3,2048]{1,0:T(4,128)S(1)} %get-tuple-element.188, f32[3,2048]{1,0:T(4,128)S(1)} %copy-done.19), kind=kLoop, calls=%fused_computation.3 | loop fusion | flops 100663296 | bytes 251707392 | tf_op jit(solution)/shard_map/convert_element_type | solution.py:115
  1063.2 20.2 %fusion.101 = bf16[4096,1,3,64]{0,3,2,1:T(8,128)(2,1)S(1)} fusion(bf16[3,2048,4096]{2,1,0:T(8,128)(2,1)} %multiply_convert_fusion.1, bf16[2048,3,32]{0,2,1:T(8,128)(2,1)} %copy-done.29, bf16[2048,3,32]{0,2,1:T(8,128)(2,1)} %copy-done.28), kind=kOutput, calls=%fused_computation.160 | convolution fusion | flops 3224371200 | bytes 52690944 | tf_op jit(solution)/shard_map/hqk,qhd->khd/dot_general | solution.py:250
  1083.4 32.6 %fusion.89 = bf16[4096,1,3,64]{0,3,2,1:T(8,128)(2,1)S(1)} fusion(bf16[2048,3,64]{0,2,1:T(8,128)(2,1)S(1)} %bitcast.362, f32[3,2048,4096]{2,1,0:T(8,128)} %get-tuple-element.182, f32[3,2048]{1,0:T(4,128)} %log_add_fusion.1), kind=kOutput, calls=%fused_computation.146 | convolution fusion | flops 3272343552 | bytes 103047168 | tf_op jit(solution)/shard_map/hqk,qhd->khd/dot_general | solution.py:253
  1118.0 23.1 %fusion.120 = f32[2048,3,64]{0,2,1:T(8,128)} fusion(bf16[3,2048,4096]{2,1,0:T(8,128)(2,1)} %multiply_convert_fusion, bf16[4096,2,3,64]{0,3,2,1:T(8,128)(2,1)} %bitcast.372), kind=kOutput, calls=%fused_computation.190 | convolution fusion | flops 3221618688 | bytes 53477376 | tf_op jit(solution)/shard_map/hqk,khd->qhd/dot_general | solution.py:246
  1141.1 22.2 %fusion.121 = f32[2048,3,64]{0,2,1:T(8,128)S(1)} fusion(bf16[3,2048,4096]{2,1,0:T(8,128)(2,1)} %multiply_convert_fusion.1, bf16[4096,2,3,64]{0,3,2,1:T(8,128)(2,1)} %bitcast.368), kind=kOutput, calls=%fused_computation.192 | convolution fusion | flops 3221618688 | bytes 53477376 | tf_op jit(solution)/shard_map/hqk,khd->qhd/dot_general | solution.py:246
  1175.1 10.3 fusion.42
  1193.5 16.4 copy.53
  1210.6 7.2 fusion.169
  1220.7 9.5 add_convert_fusion.4
  1230.5 7.5 fusion.130
  1238.1 6.8 add_convert_fusion.5
  1252.5 6.3 add_convert_fusion.6
  1259.1 172.6 %all-reduce.24.cloned.1.call-done = (bf16[2048,768]{1,0:T(8,128)(2,1)}, bf16[2048,768]{1,0:T(8,128)(2,1)}, bf16[2,2048,768]{1,0,2:T(2,128)(2,1)}) async-done(((bf16[2048,768]{1,0:T(8,128)(2,1)}, bf16[2048,768]{1,0:T(8,128)(2,1)}, bf16[2,2048,768]{1,0,2:T(2,128)(2,1)}), (bf16[2048,768]{1,0:T(8,128)(2,1)}, bf16[2048,768]{1,0:T(8,128)(2,1)}, bf16[2,2048,768]{1,0,2:T(2,128)(2,1)})) %all-reduce.24.cloned.1.call-update) | async-done | bytes 12582928 | tf_op jit(solution)/shard_map/psum | solution.py:211
  1431.8 18.3 %convert_reduce_fusion.3 = (f32[768]{0:T(1024)S(1)}, f32[768]{0:T(1024)S(1)}, f32[768]{0:T(1024)S(1)}, f32[768]{0:T(1024)S(1)}, f32[768]{0:T(1024)S(1)}, /*index...) fusion(f32[2048]{0:T(1024)S(1)} %copy-done.52, ...), kind=kLoop, calls=%fused_computation.113 | loop fusion | flops 66055680 | bytes 50381824 | tf_op jit(solution)/shard_map/reduce_sum | solution.py:221
  1457.8 61.9 %all-reduce.20.cloned.1.call-done = (f32[256,128]{1,0:T(8,128)}, f32[128,4608]{1,0:T(8,128)}) async-done(((f32[256,128]{1,0:T(8,128)}, f32[128,4608]{1,0:T(8,128)}), (f32[256,128]{1,0:T(8,128)}, f32[128,4608]{1,0:T(8,128)})) %all-reduce.20.cloned.1.call-update) | async-done | bytes 2490384 | tf_op jit(solution)/shard_map/psum | solution.py:341
  1521.2 38.9 %all-reduce.28.cloned.1.call-done = (bf16[192,576]{1,0:T(8,128)(2,1)}, bf16[192,192]{1,0:T(8,128)(2,1)}, bf16[192,768]{1,0:T(8,128)(2,1)}, bf16[768,192]{0,1:T(8,128)(2,1)}) async-done(((bf16[192,576]{1,0:T(8,128)(2,1)}, bf16[192,192]{1,0:T(8,128)(2,1)}, bf16[192,768]{1,0:T(8,128)(2,1)}, bf16[768,192]{0,1:T(8,128)(2,1)}), (bf16[192,576]{1,0:T(8,128)(2,1)}, bf16[192,192]{1,0:T(8,128)(2,1)}, ...) | async-done | bytes 884752 | tf_op jit(solution)/shard_map/psum | solution.py:322
  1586.5 24.3 %all-reduce.1 = (f32[4608]{0:T(1024)S(1)}, f32[768]{0:T(1024)S(1)}, f32[768]{0:T(1024)S(1)}, f32[3072]{0:T(1024)S(1)}, f32[768]{0:T(1024)S(1)}) all-reduce(f32[4608]{0:T(1024)S(1)} %reduce_sum.399, f32[768]{0:T(1024)S(1)} %add.365, f32[768]{0:T(1024)S(1)} %add.368, ...), channel_id=1, replica_groups=mesh['fsdp'=4,'context'=2,'tensor'=4] {'context','tensor'}, use_global_device_ids=true, to_apply=%region_51.52 | all-reduce | flops 9984 | bytes 79872 | tf_op jit(solution)/shard_map/psum | solution.py:341
  1610.8 20.7 %all-reduce.3 = (f32[4608]{0:T(1024)}, f32[768]{0:T(1024)}, f32[768]{0:T(1024)}, f32[3072]{0:T(1024)}, f32[768]{0:T(1024)}) all-reduce(f32[4608]{0:T(1024)S(1)} %get-tuple-element.107, f32[768]{0:T(1024)S(1)} %get-tuple-element.108, f32[768]{0:T(1024)S(1)} %get-tuple-element.109, ...), channel_id=1, replica_groups=mesh['fsdp'=4,'context'=2,'tensor'=4] {'fsdp'}, use_global_device_ids=true, to_apply=%region_52.53 | all-reduce | flops 9984 | bytes 79872 | tf_op jit(solution)/shard_map/psum | solution.py:340
  1637.7 25.4 %all-reduce.22.cloned.1.call-done = (f32[256,128]{1,0:T(8,128)}, f32[128,4608]{1,0:T(8,128)}) async-done(((f32[256,128]{1,0:T(8,128)}, f32[128,4608]{1,0:T(8,128)}), (f32[256,128]{1,0:T(8,128)}, f32[128,4608]{1,0:T(8,128)})) %all-reduce.22.cloned.1.call-update) | async-done | bytes 2490384 | tf_op jit(solution)/shard_map/psum | solution.py:340
  (476 shorter events, 159.4 us)
Async XLA Ops:
  8.0 105.8 %all-gather.5.cloned.1.call-start = ((), (), s32[]{:S(2)}) async-start(), calls=%async_computation.6 | async-start | bytes 4718592 | tf_op jit(solution)/shard_map/all_gather | solution.py:193
  68.9 218.8 %all-reduce.16.cloned.1.call-start = ((), (), s32[]{:S(2)}) async-start(), calls=%async_computation.7 | async-start | bytes 6291456 | tf_op jit(solution)/shard_map/psum | solution.py:200
  216.3 71.4 %copy-start.38 = (f32[768]{0:T(1024)S(1)}, f32[768]{0:T(1024)}, u32[]{:S(2)}) copy-start(f32[768]{0:T(1024)} %get-tuple-element.104) | copy-start | bytes 9220
  216.3 71.4 %copy-start.59 = (f32[2048]{0:T(1024)S(1)}, f32[2048]{0:T(1024)}, u32[]{:S(2)}) copy-start(f32[2048]{0:T(1024)} %get-tuple-element.197) | copy-start | bytes 24580
  219.1 74.8 %slice-start = ((s8[6291456]{0:T(1024)(128)(4,1)}), s8[2097152]{0:T(1024)(128)(4,1)S(1)}, s32[]{:S(2)}) async-start(s8[6291456]{0:T(1024)(128)(4,1)} %bitcast.351), calls=%async_computation.23 | async-start | bytes 4194304
  219.1 74.8 %copy-start.80 = (f32[768]{0:T(1024)S(1)}, f32[768]{0:T(1024)}, u32[]{:S(2)}) copy-start(f32[768]{0:T(1024)} %copy-done.79) | copy-start | bytes 9220
  219.1 74.8 %copy-start.93 = (f32[768]{0:T(1024)S(1)}, f32[768]{0:T(1024)}, u32[]{:S(2)}) copy-start(f32[768]{0:T(1024)} %get-tuple-element.98) | copy-start | bytes 9220
  219.1 74.8 %copy-start.123 = (f32[768]{0:T(1024)S(1)}, f32[768]{0:T(1024)}, u32[]{:S(2)}) copy-start(f32[768]{0:T(1024)} %get-tuple-element.97) | copy-start | bytes 9220
  219.1 125.3 %all-gather.11.cloned.1.call-start = ((), (), s32[]{:S(2)}) async-start(), calls=%async_computation.10 | async-start | bytes 4718592 | tf_op jit(solution)/shard_map/all_gather | solution.py:193
  297.8 46.6 %copy-start.30 = (bf16[2048,3,32]{0,2,1:T(8,128)(2,1)}, bf16[2048,3,32]{0,2,1:T(8,128)(2,1)S(1)}, u32[]{:S(2)}) copy-start(bf16[2048,3,32]{0,2,1:T(8,128)(2,1)S(1)} %get-tuple-element.154) | copy-start | bytes 1179652
  297.8 46.6 %copy-start.31 = (bf16[2048,3,32]{0,2,1:T(8,128)(2,1)}, bf16[2048,3,32]{0,2,1:T(8,128)(2,1)S(1)}, u32[]{:S(2)}) copy-start(bf16[2048,3,32]{0,2,1:T(8,128)(2,1)S(1)} %get-tuple-element.155) | copy-start | bytes 1179652
  299.2 221.1 %all-reduce.18.cloned.1.call-start = ((), (), s32[]{:S(2)}) async-start(), calls=%async_computation.11 | async-start | bytes 6291456 | tf_op jit(solution)/shard_map/psum | solution.py:200
  447.5 72.8 %copy-start.39 = (f32[768]{0:T(1024)S(1)}, f32[768]{0:T(1024)}, u32[]{:S(2)}) copy-start(f32[768]{0:T(1024)} %get-tuple-element.104) | copy-start | bytes 9220
  447.5 72.8 %copy-start.41 = (f32[768]{0:T(1024)S(1)}, f32[768]{0:T(1024)}, u32[]{:S(2)}) copy-start(f32[768]{0:T(1024)} %get-tuple-element.99) | copy-start | bytes 9220
  447.5 79.4 %slice-start.2 = ((s8[6291456]{0:T(1024)(128)(4,1)}), s8[2097152]{0:T(1024)(128)(4,1)S(1)}, s32[]{:S(2)}) async-start(s8[6291456]{0:T(1024)(128)(4,1)} %bitcast.353), calls=%async_computation.25 | async-start | bytes 4194304
  451.7 77.2 %all-gather.7.cloned.1.call-start = ((), (), s32[]{:S(2)}) async-start(), calls=%async_computation.8 | async-start | bytes 1474560 | tf_op jit(solution)/shard_map/all_gather | solution.py:138
  452.3 86.5 %all-gather.9.cloned.1.call-start = ((), (), s32[]{:S(2)}) async-start(), calls=%async_computation.9 | async-start | bytes 1474560 | tf_op jit(solution)/shard_map/all_gather | solution.py:140
  452.8 251.1 %all-reduce.26.cloned.1.call-start = ((), (), s32[]{:S(2)}) async-start(), calls=%async_computation.21 | async-start | bytes 12582912 | tf_op jit(solution)/shard_map/psum | solution.py:233
  452.9 251.1 %copy-start.51 = (f32[2048]{0:T(1024)}, f32[2048]{0:T(1024)S(1)}, u32[]{:S(2)}) copy-start(f32[2048]{0:T(1024)S(1)} %compare_convert_fusion.1) | copy-start | bytes 24580
  452.9 251.0 %copy-start.53 = (f32[2048]{0:T(1024)}, f32[2048]{0:T(1024)S(1)}, u32[]{:S(2)}) copy-start(f32[2048]{0:T(1024)S(1)} %compare_convert_fusion) | copy-start | bytes 24580
  453.0 123.4 %copy-start.95 = (f32[768]{0:T(1024)}, f32[768]{0:T(1024)S(1)}, u32[]{:S(2)}) copy-start(f32[768]{0:T(1024)S(1)} %convert_element_type.335) | copy-start | bytes 9220
  453.8 138.3 %copy-start.119 = (f32[768]{0:T(1024)}, f32[768]{0:T(1024)S(1)}, u32[]{:S(2)}) copy-start(f32[768]{0:T(1024)S(1)} %dynamic-slice_convert_fusion) | copy-start | bytes 9220
  453.8 122.6 %copy-start.65 = (f32[2048]{0:T(1024)}, f32[2048]{0:T(1024)S(1)}, u32[]{:S(2)}) copy-start(f32[2048]{0:T(1024)S(1)} %broadcast_multiply_fusion.12) | copy-start | bytes 24580
  527.1 49.3 %copy-start.67 = (f32[2048]{0:T(1024)}, f32[2048]{0:T(1024)S(1)}, u32[]{:S(2)}) copy-start(f32[2048]{0:T(1024)S(1)} %broadcast_multiply_fusion.10) | copy-start | bytes 24580
  528.8 47.6 %copy-start.77 = (f32[2048]{0:T(1024)}, f32[2048]{0:T(1024)S(1)}, u32[]{:S(2)}) copy-start(f32[2048]{0:T(1024)S(1)} %add_rsqrt_fusion.2) | copy-start | bytes 24580
  528.9 47.5 %copy-start.75 = (f32[2048]{0:T(1024)}, f32[2048]{0:T(1024)S(1)}, u32[]{:S(2)}) copy-start(f32[2048]{0:T(1024)S(1)} %add_rsqrt_fusion) | copy-start | bytes 24580
  583.9 579.4 %reduce-scatter.11.cloned.1.call-start = ((), (), s32[]{:S(2)}) async-start(), calls=%async_computation.13 | async-start | bytes 4718592 | tf_op jit(solution)/shard_map/reduce_scatter | solution.py:260
  917.9 248.6 %reduce-scatter.9.cloned.1.call-start = ((), (), s32[]{:S(2)}) async-start(), calls=%async_computation.12 | async-start | bytes 4718592 | tf_op jit(solution)/shard_map/reduce_scatter | solution.py:260
  917.9 67.6 %copy-start.19 = (f32[3,2048]{1,0:T(4,128)S(1)}, f32[3,2048]{1,0:T(4,128)}, u32[]{:S(2)}) copy-start(f32[3,2048]{1,0:T(4,128)} %log_add_fusion.1) | copy-start | bytes 73732
  1117.9 313.8 %all-reduce.24.cloned.1.call-start = ((), (), s32[]{:S(2)}) async-start(), calls=%async_computation.20 | async-start | bytes 25165824 | tf_op jit(solution)/shard_map/psum | solution.py:211
  1210.0 246.1 %reduce-scatter.19.cloned.1.call-start = ((), (), s32[]{:S(2)}) async-start(), calls=%async_computation.17 | async-start | bytes 491520
  1220.4 237.3 %reduce-scatter.17.cloned.1.call-start = ((), (), s32[]{:S(2)}) async-start(), calls=%async_computation.16 | async-start | bytes 1474560 | tf_op jit(solution)/shard_map/reduce_scatter | solution.py:317
  1230.3 227.4 %reduce-scatter.15.cloned.1.call-start = ((), (), s32[]{:S(2)}) async-start(), calls=%async_computation.15 | async-start | bytes 1474560 | tf_op jit(solution)/shard_map/reduce_scatter | solution.py:311
  1244.9 212.9 %reduce-scatter.13.cloned.1.call-start = ((), (), s32[]{:S(2)}) async-start(), calls=%async_computation.14 | async-start | bytes 1228800 | tf_op jit(solution)/shard_map/reduce_scatter | solution.py:308
  1252.5 179.2 %copy-start.55 = (f32[2048]{0:T(1024)S(1)}, f32[2048]{0:T(1024)}, u32[]{:S(2)}) copy-start(f32[2048]{0:T(1024)} %copy-done.53) | copy-start | bytes 24580
  1252.5 179.2 %copy-start.83 = (f32[768]{0:T(1024)S(1)}, f32[768]{0:T(1024)}, u32[]{:S(2)}) copy-start(f32[768]{0:T(1024)} %convert_element_type.341) | copy-start | bytes 9220
  1252.5 179.2 %copy-start.86 = (f32[768]{0:T(1024)S(1)}, f32[768]{0:T(1024)}, u32[]{:S(2)}) copy-start(f32[768]{0:T(1024)} %get-tuple-element.93) | copy-start | bytes 9220
  1252.5 179.2 %copy-start.89 = (f32[768]{0:T(1024)S(1)}, f32[768]{0:T(1024)}, u32[]{:S(2)}) copy-start(f32[768]{0:T(1024)} %get-tuple-element.96) | copy-start | bytes 9220
  1258.9 260.8 %all-reduce.20.cloned.1.call-start = ((), (), s32[]{:S(2)}) async-start(), calls=%async_computation.18 | async-start | bytes 4980736 | tf_op jit(solution)/shard_map/psum | solution.py:341
  1450.0 69.7 %copy-start.135 = (u32[32]{0:T(128)S(1)}, u32[32]{0:T(128)}, u32[]{:S(2)}) copy-start(u32[32]{0:T(128)} %constant.93) | copy-start | bytes 388
  1450.1 71.0 %copy-start.107 = (f32[768]{0:T(1024)S(1)}, f32[768]{0:T(1024)}, u32[]{:S(2)}) copy-start(f32[768]{0:T(1024)} %get-tuple-element.52) | copy-start | bytes 9220
  1450.1 71.0 %copy-start.108 = (f32[768]{0:T(1024)S(1)}, f32[768]{0:T(1024)}, u32[]{:S(2)}) copy-start(f32[768]{0:T(1024)} %get-tuple-element.80) | copy-start | bytes 9220
  1450.1 71.0 %copy-start.105 = (f32[768]{0:T(1024)S(1)}, f32[768]{0:T(1024)}, u32[]{:S(2)}) copy-start(f32[768]{0:T(1024)} %get-tuple-element.193) | copy-start | bytes 9220
  1450.1 71.0 %copy-start.106 = (f32[768]{0:T(1024)S(1)}, f32[768]{0:T(1024)}, u32[]{:S(2)}) copy-start(f32[768]{0:T(1024)} %get-tuple-element.195) | copy-start | bytes 9220
  1450.1 71.1 %copy-start.109 = (f32[768]{0:T(1024)S(1)}, f32[768]{0:T(1024)}, u32[]{:S(2)}) copy-start(f32[768]{0:T(1024)} %get-tuple-element.58) | copy-start | bytes 9220
  1450.1 71.1 %copy-start.110 = (f32[768]{0:T(1024)S(1)}, f32[768]{0:T(1024)}, u32[]{:S(2)}) copy-start(f32[768]{0:T(1024)} %get-tuple-element.84) | copy-start | bytes 9220
  1455.9 104.3 %all-reduce.28.cloned.1.call-start = ((), (), s32[]{:S(2)}) async-start(), calls=%async_computation.22 | async-start | bytes 1867776 | tf_op jit(solution)/shard_map/psum | solution.py:322
  1457.8 205.3 %all-reduce.22.cloned.1.call-start = ((), (), s32[]{:S(2)}) async-start(), calls=%async_computation.19 | async-start | bytes 4980736 | tf_op jit(solution)/shard_map/psum | solution.py:340
  (118 other events, 1016.4 us)
Sparse Core Ops, SparseCore 0:
  69.0 44.7 all-gather.4
  219.2 68.4 all-reduce.15
  299.4 45.0 all-gather.10
  451.8 68.4 all-reduce.17
  584.1 119.8 all-reduce.25
  918.0 43.5 reduce-scatter.10
  1118.0 43.5 reduce-scatter.8
  1210.1 221.5 all-reduce.23
Sparse Core Ops, SparseCore 1:
  453.7 30.2 all-gather.6
  485.4 29.4 all-gather.8
  1220.5 20.8 reduce-scatter.18
  1243.7 27.3 reduce-scatter.16
  1273.5 27.8 reduce-scatter.14
  1303.8 24.7 reduce-scatter.12
  1455.9 63.7 all-reduce.19
  1522.8 37.3 all-reduce.27
  1562.5 100.5 all-reduce.21
